TPU v7x, 256 devices: a whole 4x4x8 slice. The times are simulated.
256 devices in a mesh: row: 16 (over z, core), col: 16 (over y, x).
Axes of the slice: x: 4, y: 4, z: 8, core: 2. Of those that a mesh axis runs over, the one named last changes fastest.
Arguments:
- momentum: float32 [8192, 26624], P('row', 'col'), may hold values from -20 to 20
- grad: bfloat16 [8192, 26624], P('row', 'col'), may hold values from -3 to 3
- basis: float32 [26624, 128], P('col'), may hold values from -0.0390625 to 0.0390625
Outputs:
- momentum_out: float32 [8192, 26624], P('row', 'col')
- left_out: float32 [2, 8192, 128], P(None, 'row')
- right_out: float32 [26624, 128], P('col')
All inputs are finite; a program needn't handle non-finite values.
Results may differ from a plain program's by a relative error of at most 0.0003.
Values sent between devices are 32-bit elements; how exact they have to be, the bound alone decides.
A program may use at most 64 MiB of HBM per device.

v0:
```python
import jax
import jax.numpy as jnp
from jax import lax
from jax.sharding import PartitionSpec as P

ITERS = 2


def chol_solve(share, gram):
    lower = jnp.linalg.cholesky(gram)
    return jax.scipy.linalg.solve_triangular(lower, share.T, lower=True).T


def gram_of(share):
    return lax.dot_general(share, share, (((0,), (0,)), ((), ())), precision=lax.Precision.HIGHEST)


def shards(momentum, grad, basis):
    work = momentum + grad.astype(jnp.float32)
    row_count = momentum.shape[0]
    col_count = momentum.shape[1]
    total_rows = row_count * lax.axis_size("row")
    total_cols = col_count * lax.axis_size("col")
    lefts = []
    for step in range(ITERS):
        current = work
        current_basis = basis
        proj = lax.psum(jnp.dot(current, current_basis, precision=lax.Precision.HIGHEST), "col")
        gram_left = lax.psum(gram_of(proj), "row")
        left = chol_solve(proj, gram_left)
        partial_right = lax.dot_general(
            current, left, (((0,), (0,)), ((), ())), precision=lax.Precision.HIGHEST
        )
        right_raw = lax.psum(partial_right, "row")
        gram_right = lax.psum(gram_of(right_raw), "col")
        basis = chol_solve(right_raw, gram_right)
        outer = lax.dot_general(
            left, right_raw, (((1,), (1,)), ((), ())), precision=lax.Precision.HIGHEST
        )
        work = current - 0.95 * outer
        lefts.append(left * jnp.sqrt(jnp.float32(total_rows)))
    return (work, jnp.stack(lefts), basis * jnp.sqrt(jnp.float32(total_cols)))


def solution(mesh):
    in_specs = (P("row", "col"), P("row", "col"), P("col", None))
    out_specs = (P("row", "col"), P(None, "row", None), P("col", None))
    return jax.shard_map(shards, mesh=mesh, in_specs=in_specs, out_specs=out_specs, check_vma=False)
```

profile of v0, /device:TPU:2, one launch (start us, length us, event | category | flops | bytes accessed | tf_op | source)
XLA Modules:
  0.0 950.0 jit_solution(10892102189534766534)
XLA Ops:
  8.3 6.2 fusion.2
  14.6 97.0 %all-reduce.9.cloned.1.call-done = f32[512,128]{1,0:T(8,128)} async-done(((f32[512,128]{1,0:T(8,128)}), f32[512,128]{1,0:T(8,128)}) %all-reduce.9.cloned.1.call-update) | async-done | bytes 262160 | tf_op jit(solution)/shard_map/psum | solution.py:28
  114.1 99.1 %all-reduce.11.cloned.1.call-done = f32[128,128]{0,1:T(8,128)} async-done(((f32[128,128]{0,1:T(8,128)}), f32[128,128]{0,1:T(8,128)}) %all-reduce.11.cloned.1.call-update) | async-done | bytes 65552 | tf_op jit(solution)/shard_map/psum | solution.py:29
  214.9 11.7 %cholesky.74 = f32[128,128]{1,0:T(8,128)S(1)} custom-call(f32[128,128]{1,0:T(8,128)S(1)} %fusion.21), custom_call_target="Cholesky" | custom-call | tf_op jit(solution)/shard_map/jit(cholesky)/cholesky | solution.py:10
  228.0 9.8 %custom-call.10 = f32[1,128,128]{1,2,0:T(8,128)S(1)} custom-call(f32[1,128,128]{2,1,0:T(8,128)S(1)} %fusion.10), custom_call_target="InvertDiagBlocksLowerTriangular" | custom-call | tf_op jit(solution)/shard_map/jit(_solve_triangular)/triangular_solve | solution.py:11
  239.9 8.3 fusion.1
  248.3 109.5 %all-reduce.13.cloned.1.call-done = f32[1664,128]{1,0:T(8,128)} async-done(((f32[1664,128]{1,0:T(8,128)}), f32[1664,128]{1,0:T(8,128)}) %all-reduce.13.cloned.1.call-update) | async-done | bytes 851984 | tf_op jit(solution)/shard_map/psum | solution.py:34
  357.8 3.5 fusion.23
  361.8 7.3 multiply_subtract_fusion.1
  369.2 82.3 %all-reduce.15.cloned.1.call-done = f32[128,128]{0,1:T(8,128)} async-done(((f32[128,128]{0,1:T(8,128)}), f32[128,128]{0,1:T(8,128)}) %all-reduce.15.cloned.1.call-update) | async-done | bytes 65552 | tf_op jit(solution)/shard_map/psum | solution.py:35
  453.3 11.7 %cholesky.85 = f32[128,128]{1,0:T(8,128)S(1)} custom-call(f32[128,128]{1,0:T(8,128)S(1)} %fusion.19), custom_call_target="Cholesky" | custom-call | tf_op jit(solution)/shard_map/jit(cholesky)/cholesky | solution.py:10
  466.4 9.8 %custom-call.11 = f32[1,128,128]{1,2,0:T(8,128)S(1)} custom-call(f32[1,128,128]{2,1,0:T(8,128)S(1)} %fusion.11), custom_call_target="InvertDiagBlocksLowerTriangular" | custom-call | tf_op jit(solution)/shard_map/jit(_solve_triangular)/triangular_solve | solution.py:11
  477.1 5.8 fusion.24
  483.0 93.9 %all-reduce.17.cloned.1.call-done = f32[512,128]{1,0:T(8,128)} async-done(((f32[512,128]{1,0:T(8,128)}), f32[512,128]{1,0:T(8,128)}) %all-reduce.17.cloned.1.call-update) | async-done | bytes 262160 | tf_op jit(solution)/shard_map/psum | solution.py:28
  579.2 99.1 %all-reduce.19.cloned.1.call-done = f32[128,128]{0,1:T(8,128)} async-done(((f32[128,128]{0,1:T(8,128)}), f32[128,128]{0,1:T(8,128)}) %all-reduce.19.cloned.1.call-update) | async-done | bytes 65552 | tf_op jit(solution)/shard_map/psum | solution.py:29
  680.0 11.7 %cholesky.96 = f32[128,128]{1,0:T(8,128)S(1)} custom-call(f32[128,128]{1,0:T(8,128)S(1)} %fusion.17), custom_call_target="Cholesky" | custom-call | tf_op jit(solution)/shard_map/jit(cholesky)/cholesky | solution.py:10
  693.1 9.8 %custom-call.12 = f32[1,128,128]{1,2,0:T(8,128)S(1)} custom-call(f32[1,128,128]{2,1,0:T(8,128)S(1)} %fusion.12), custom_call_target="InvertDiagBlocksLowerTriangular" | custom-call | tf_op jit(solution)/shard_map/jit(_solve_triangular)/triangular_solve | solution.py:11
  704.3 8.3 fusion.26
  714.0 108.2 %all-reduce.21.cloned.1.call-done = f32[1664,128]{1,0:T(8,128)} async-done(((f32[1664,128]{1,0:T(8,128)}), f32[1664,128]{1,0:T(8,128)}) %all-reduce.21.cloned.1.call-update) | async-done | bytes 851984 | tf_op jit(solution)/shard_map/psum | solution.py:34
  822.2 3.5 fusion.27
  825.8 6.4 multiply_subtract_fusion
  832.1 83.9 %all-reduce.23.cloned.1.call-done = f32[128,128]{0,1:T(8,128)} async-done(((f32[128,128]{0,1:T(8,128)}), f32[128,128]{0,1:T(8,128)}) %all-reduce.23.cloned.1.call-update) | async-done | bytes 65552 | tf_op jit(solution)/shard_map/psum | solution.py:35
  917.9 11.7 %cholesky.107 = f32[128,128]{1,0:T(8,128)S(1)} custom-call(f32[128,128]{1,0:T(8,128)S(1)} %fusion.15), custom_call_target="Cholesky" | custom-call | tf_op jit(solution)/shard_map/jit(cholesky)/cholesky | solution.py:10
  930.9 9.8 %custom-call.13 = f32[1,128,128]{1,2,0:T(8,128)S(1)} custom-call(f32[1,128,128]{2,1,0:T(8,128)S(1)} %fusion.13), custom_call_target="InvertDiagBlocksLowerTriangular" | custom-call | tf_op jit(solution)/shard_map/jit(_solve_triangular)/triangular_solve | solution.py:11
  (59 shorter events, 27.0 us)
Async XLA Ops:
  7.2 1.2 copy-start
  7.2 232.7 %copy-start.1 = (bf16[512,1664]{1,0:T(8,128)(2,1)S(1)}, bf16[512,1664]{1,0:T(8,128)(2,1)}, u32[]{:S(2)}) copy-start(bf16[512,1664]{1,0:T(8,128)(2,1)} %param.9) | copy-start | bytes 5111812
  7.2 104.4 %all-reduce.9.cloned.1.call-start = ((), (), s32[]{:S(2)}) async-start(), calls=%async_computation | async-start | bytes 524288 | tf_op jit(solution)/shard_map/psum | solution.py:28
  14.5 198.6 %all-reduce.11.cloned.1.call-start = ((), (), s32[]{:S(2)}) async-start(), calls=%async_computation.1 | async-start | bytes 131072 | tf_op jit(solution)/shard_map/psum | solution.py:29
  113.8 244.0 %all-reduce.13.cloned.1.call-start = ((), (), s32[]{:S(2)}) async-start(), calls=%async_computation.2 | async-start | bytes 1703936 | tf_op jit(solution)/shard_map/psum | solution.py:34
  239.1 0.7 copy-start.4
  248.2 203.3 %all-reduce.15.cloned.1.call-start = ((), (), s32[]{:S(2)}) async-start(), calls=%async_computation.3 | async-start | bytes 131072 | tf_op jit(solution)/shard_map/psum | solution.py:35
  361.4 114.8 %copy-start.2 = (f32[1664,128]{1,0:T(8,128)S(1)}, f32[1664,128]{1,0:T(8,128)}, u32[]{:S(2)}) copy-start(f32[1664,128]{1,0:T(8,128)} %all-reduce.13.cloned.1.call-done) | copy-start | bytes 2555908
  361.4 215.5 %all-reduce.17.cloned.1.call-start = ((), (), s32[]{:S(2)}) async-start(), calls=%async_computation.4 | async-start | bytes 524288 | tf_op jit(solution)/shard_map/psum | solution.py:28
  482.9 195.3 %all-reduce.19.cloned.1.call-start = ((), (), s32[]{:S(2)}) async-start(), calls=%async_computation.5 | async-start | bytes 131072 | tf_op jit(solution)/shard_map/psum | solution.py:29
  579.1 133.8 %copy-start.5 = (f32[128,512]{1,0:T(8,128)S(1)}, f32[128,512]{1,0:T(8,128)}, u32[]{:S(2)}) copy-start(f32[128,512]{1,0:T(8,128)} %copy-done.4) | copy-start | bytes 786436
  579.1 243.1 %all-reduce.21.cloned.1.call-start = ((), (), s32[]{:S(2)}) async-start(), calls=%async_computation.6 | async-start | bytes 1703936 | tf_op jit(solution)/shard_map/psum | solution.py:34
  712.7 203.4 %all-reduce.23.cloned.1.call-start = ((), (), s32[]{:S(2)}) async-start(), calls=%async_computation.7 | async-start | bytes 131072 | tf_op jit(solution)/shard_map/psum | solution.py:35
  825.8 115.0 %copy-start.3 = (f32[1664,128]{1,0:T(8,128)S(1)}, f32[1664,128]{1,0:T(8,128)}, u32[]{:S(2)}) copy-start(f32[1664,128]{1,0:T(8,128)} %all-reduce.21.cloned.1.call-done) | copy-start | bytes 2555908
Sparse Core Ops, SparseCore 0:
  14.6 96.8 all-reduce.8
  114.6 98.5 all-reduce.10
  248.3 109.3 all-reduce.12
  361.7 89.7 all-reduce.14
  483.1 93.7 all-reduce.16
  579.7 98.5 all-reduce.18
  712.8 109.3 all-reduce.20
  826.3 89.7 all-reduce.22
where the time goes:
time: 954 us; the launch traced here: 950 us
  waiting for transfers between devices  773 us (81%)
  other arithmetic  94.9 us (10%)
  matrix products  58.6 us (6%)
  between operations  14.6 us (2%)
    psum x2, waiting for transfers between devices, shards(): right_raw = lax.psum(partial_right, 'row')  218 us
    psum x2, waiting for transfers between devices, shards(): gram_left = lax.psum(gram_of(proj), 'row')  198 us
    psum x2, waiting for transfers between devices, shards(): lax.psum(jnp.dot(current, current_basis, precision=lax.Precision.HIGHEST)...  191 us
    psum x2, waiting for transfers between devices, shards(): gram_right = lax.psum(gram_of(right_raw), 'col')  166 us
    another operation x12, other arithmetic, chol_solve(): lower = jnp.linalg.cholesky(gram)  49.6 us
    another operation x8, other arithmetic, chol_solve(): return jax.scipy.linalg.solve_triangular(lower, share.T, lower=True).T  41.9 us
  transfers between devices with their start and end apart: 8, of which 8 were waited for; matrix products, arithmetic and copies ran while one was open for 2% of the time, Pallas kernels for 0%

commit v1 on v0

--- a/solution.py
+++ b/solution.py
@@ -31,7 +31,7 @@
         partial_right = lax.dot_general(
             current, left, (((0,), (0,)), ((), ())), precision=lax.Precision.HIGHEST
         )
-        right_raw = lax.psum(partial_right, "row")
+        right_raw = jnp.sum(lax.all_gather(partial_right, "row"), axis=0)
         gram_right = lax.psum(gram_of(right_raw), "col")
         basis = chol_solve(right_raw, gram_right)
         outer = lax.dot_general(

time: 954 us -> 901 us (0.944)
  waiting for transfers between devices: 773 us -> 712 us
  other arithmetic: 94.9 us -> 106 us
    psum x2 -> x0, waiting for transfers between devices: 218 us -> none  [shards(): right_raw = lax.psum(partial_right, 'row')]
    all_gather x0 -> x2, waiting for transfers between devices: none -> 157 us  [shards(): right_raw = jnp.sum(lax.all_gather(partial_right, 'row'), axis=0)]
    reduce_sum x0 -> x2, other arithmetic: none -> 11.2 us  [shards(): right_raw = jnp.sum(lax.all_gather(partial_right, 'row'), axis=0)]
where the time goes in v1:
time: 901 us; the launch traced here: 896 us
  waiting for transfers between devices  712 us (79%)
  other arithmetic  106 us (12%)
  matrix products  55.2 us (6%)
  between operations  14.6 us (2%)
    psum x2, waiting for transfers between devices, shards(): gram_left = lax.psum(gram_of(proj), 'row')  198 us
    psum x2, waiting for transfers between devices, shards(): lax.psum(jnp.dot(current, current_basis, precision=lax.Precision.HIGHEST)...  191 us
    psum x2, waiting for transfers between devices, shards(): gram_right = lax.psum(gram_of(right_raw), 'col')  165 us
    all_gather x2, waiting for transfers between devices, shards(): right_raw = jnp.sum(lax.all_gather(partial_right, 'row'), axis=0)  157 us
    another operation x12, other arithmetic, chol_solve(): lower = jnp.linalg.cholesky(gram)  49.6 us
    another operation x8, other arithmetic, chol_solve(): return jax.scipy.linalg.solve_triangular(lower, share.T, lower=True).T  41.9 us
  transfers between devices with their start and end apart: 8, of which 8 were waited for; matrix products, arithmetic and copies ran while one was open for 2% of the time, Pallas kernels for 0%

profile of v1, /device:TPU:2, one launch (start us, length us, event | category | flops | bytes accessed | tf_op | source)
XLA Modules:
  0.0 896.4 jit_solution(17928005339979533061)
XLA Ops:
  8.3 6.2 fusion.2
  14.6 97.0 %all-reduce.7.cloned.1.call-done = f32[512,128]{1,0:T(8,128)} async-done(((f32[512,128]{1,0:T(8,128)}), f32[512,128]{1,0:T(8,128)}) %all-reduce.7.cloned.1.call-update) | async-done | bytes 262160 | tf_op jit(solution)/shard_map/psum | solution.py:28
  114.1 99.1 %all-reduce.9.cloned.1.call-done = f32[128,128]{0,1:T(8,128)} async-done(((f32[128,128]{0,1:T(8,128)}), f32[128,128]{0,1:T(8,128)}) %all-reduce.9.cloned.1.call-update) | async-done | bytes 65552 | tf_op jit(solution)/shard_map/psum | solution.py:29
  214.9 11.7 %cholesky.74 = f32[128,128]{1,0:T(8,128)S(1)} custom-call(f32[128,128]{1,0:T(8,128)S(1)} %fusion.21), custom_call_target="Cholesky" | custom-call | tf_op jit(solution)/shard_map/jit(cholesky)/cholesky | solution.py:10
  228.0 9.8 %custom-call.10 = f32[1,128,128]{1,2,0:T(8,128)S(1)} custom-call(f32[1,128,128]{2,1,0:T(8,128)S(1)} %fusion.10), custom_call_target="InvertDiagBlocksLowerTriangular" | custom-call | tf_op jit(solution)/shard_map/jit(_solve_triangular)/triangular_solve | solution.py:11
  239.9 8.3 fusion.1
  248.3 79.4 %all-gather.5.cloned.1.call-done = f32[26624,128]{1,0:T(8,128)} async-done(((f32[1664,128]{1,0:T(8,128)}), f32[26624,128]{1,0:T(8,128)}) %all-gather.5.cloned.1.call-update) | async-done | bytes 13631504 | tf_op jit(solution)/shard_map/all_gather | solution.py:34
  327.7 5.6 reduce_sum.18
  335.9 7.1 multiply_subtract_fusion.1
  343.0 81.9 %all-reduce.11.cloned.1.call-done = f32[128,128]{0,1:T(8,128)} async-done(((f32[128,128]{0,1:T(8,128)}), f32[128,128]{0,1:T(8,128)}) %all-reduce.11.cloned.1.call-update) | async-done | bytes 65552 | tf_op jit(solution)/shard_map/psum | solution.py:35
  426.6 11.7 %cholesky.85 = f32[128,128]{1,0:T(8,128)S(1)} custom-call(f32[128,128]{1,0:T(8,128)S(1)} %fusion.19), custom_call_target="Cholesky" | custom-call | tf_op jit(solution)/shard_map/jit(cholesky)/cholesky | solution.py:10
  439.7 9.8 %custom-call.11 = f32[1,128,128]{1,2,0:T(8,128)S(1)} custom-call(f32[1,128,128]{2,1,0:T(8,128)S(1)} %fusion.11), custom_call_target="InvertDiagBlocksLowerTriangular" | custom-call | tf_op jit(solution)/shard_map/jit(_solve_triangular)/triangular_solve | solution.py:11
  450.5 5.8 fusion.24
  456.3 93.9 %all-reduce.13.cloned.1.call-done = f32[512,128]{1,0:T(8,128)} async-done(((f32[512,128]{1,0:T(8,128)}), f32[512,128]{1,0:T(8,128)}) %all-reduce.13.cloned.1.call-update) | async-done | bytes 262160 | tf_op jit(solution)/shard_map/psum | solution.py:28
  552.5 99.0 %all-reduce.15.cloned.1.call-done = f32[128,128]{0,1:T(8,128)} async-done(((f32[128,128]{0,1:T(8,128)}), f32[128,128]{0,1:T(8,128)}) %all-reduce.15.cloned.1.call-update) | async-done | bytes 65552 | tf_op jit(solution)/shard_map/psum | solution.py:29
  653.3 11.7 %cholesky.96 = f32[128,128]{1,0:T(8,128)S(1)} custom-call(f32[128,128]{1,0:T(8,128)S(1)} %fusion.17), custom_call_target="Cholesky" | custom-call | tf_op jit(solution)/shard_map/jit(cholesky)/cholesky | solution.py:10
  666.4 9.8 %custom-call.12 = f32[1,128,128]{1,2,0:T(8,128)S(1)} custom-call(f32[1,128,128]{2,1,0:T(8,128)S(1)} %fusion.12), custom_call_target="InvertDiagBlocksLowerTriangular" | custom-call | tf_op jit(solution)/shard_map/jit(_solve_triangular)/triangular_solve | solution.py:11
  677.6 8.3 fusion.26
  687.3 78.1 %all-gather.7.cloned.1.call-done = f32[26624,128]{1,0:T(8,128)} async-done(((f32[1664,128]{1,0:T(8,128)}), f32[26624,128]{1,0:T(8,128)}) %all-gather.7.cloned.1.call-update) | async-done | bytes 13631504 | tf_op jit(solution)/shard_map/all_gather | solution.py:34
  765.4 5.6 reduce_sum.19
  773.1 6.1 multiply_subtract_fusion
  779.2 83.3 %all-reduce.17.cloned.1.call-done = f32[128,128]{0,1:T(8,128)} async-done(((f32[128,128]{0,1:T(8,128)}), f32[128,128]{0,1:T(8,128)}) %all-reduce.17.cloned.1.call-update) | async-done | bytes 65552 | tf_op jit(solution)/shard_map/psum | solution.py:35
  864.3 11.7 %cholesky.107 = f32[128,128]{1,0:T(8,128)S(1)} custom-call(f32[128,128]{1,0:T(8,128)S(1)} %fusion.15), custom_call_target="Cholesky" | custom-call | tf_op jit(solution)/shard_map/jit(cholesky)/cholesky | solution.py:10
  877.4 9.8 %custom-call.13 = f32[1,128,128]{1,2,0:T(8,128)S(1)} custom-call(f32[1,128,128]{2,1,0:T(8,128)S(1)} %fusion.13), custom_call_target="InvertDiagBlocksLowerTriangular" | custom-call | tf_op jit(solution)/shard_map/jit(_solve_triangular)/triangular_solve | solution.py:11
  (57 shorter events, 31.2 us)
Async XLA Ops:
  7.2 1.2 copy-start
  7.2 232.7 %copy-start.1 = (bf16[512,1664]{1,0:T(8,128)(2,1)S(1)}, bf16[512,1664]{1,0:T(8,128)(2,1)}, u32[]{:S(2)}) copy-start(bf16[512,1664]{1,0:T(8,128)(2,1)} %param.9) | copy-start | bytes 5111812
  7.2 104.4 %all-reduce.7.cloned.1.call-start = ((), (), s32[]{:S(2)}) async-start(), calls=%async_computation | async-start | bytes 524288 | tf_op jit(solution)/shard_map/psum | solution.py:28
  14.5 198.6 %all-reduce.9.cloned.1.call-start = ((), (), s32[]{:S(2)}) async-start(), calls=%async_computation.1 | async-start | bytes 131072 | tf_op jit(solution)/shard_map/psum | solution.py:29
  113.8 213.9 %all-gather.5.cloned.1.call-start = ((), (), s32[]{:S(2)}) async-start(), calls=%async_computation.6 | async-start | bytes 14483456 | tf_op jit(solution)/shard_map/all_gather | solution.py:34
  239.1 0.7 copy-start.2
  248.2 176.6 %all-reduce.11.cloned.1.call-start = ((), (), s32[]{:S(2)}) async-start(), calls=%async_computation.2 | async-start | bytes 131072 | tf_op jit(solution)/shard_map/psum | solution.py:35
  335.4 214.8 %all-reduce.13.cloned.1.call-start = ((), (), s32[]{:S(2)}) async-start(), calls=%async_computation.3 | async-start | bytes 524288 | tf_op jit(solution)/shard_map/psum | solution.py:28
  456.3 195.2 %all-reduce.15.cloned.1.call-start = ((), (), s32[]{:S(2)}) async-start(), calls=%async_computation.4 | async-start | bytes 131072 | tf_op jit(solution)/shard_map/psum | solution.py:29
  552.4 133.7 %copy-start.3 = (f32[128,512]{1,0:T(8,128)S(1)}, f32[128,512]{1,0:T(8,128)}, u32[]{:S(2)}) copy-start(f32[128,512]{1,0:T(8,128)} %copy-done.2) | copy-start | bytes 786436
  552.5 212.9 %all-gather.7.cloned.1.call-start = ((), (), s32[]{:S(2)}) async-start(), calls=%async_computation.7 | async-start | bytes 14483456 | tf_op jit(solution)/shard_map/all_gather | solution.py:34
  685.9 176.6 %all-reduce.17.cloned.1.call-start = ((), (), s32[]{:S(2)}) async-start(), calls=%async_computation.5 | async-start | bytes 131072 | tf_op jit(solution)/shard_map/psum | solution.py:35
Sparse Core Ops, SparseCore 0:
  14.6 96.8 all-reduce.6
  114.6 98.5 all-reduce.8
  248.3 79.2 all-gather.4
  335.6 89.2 all-reduce.10
  456.4 93.7 all-reduce.12
  552.9 98.5 all-reduce.14
  686.0 79.2 all-gather.6
  773.2 89.2 all-reduce.16
